TPU v7x, 32 devices: a whole 2x2x4 slice. The times are simulated.
32 devices in a mesh: grp: 2 (over y), mesh: 4 (over z), chaos: 2 (over x), kl: 2 (over core).
Axes of the slice: x: 2, y: 2, z: 4, core: 2. Of those that a mesh axis runs over, the one named last changes fastest.
Arguments:
- right_side: float32 [44, 2048], P(('grp', 'chaos'), 'mesh'), parts along dimension 0, may hold values from -14 to 14
- preconditioner: float32 [22, 2048], P('chaos', 'mesh'), may hold values from 0.15 to 0.6
- mass_diag: float32 [2048], P('mesh'), may hold values from 0.5 to 2
- halo_lists: int32 [2, 256], P(None, 'mesh'), may hold values from 0 to 511, as said below
- connectivity: int32 [4, 10240], P(None, 'mesh'), may hold values from 0 to 639
- gradients: float32 [3, 4, 10240], P(None, None, 'mesh'), may hold values from -0.9 to 0.9
- coefficient: float32 [20, 10240], P(('grp', 'kl'), 'mesh'), parts along dimension 0, may hold values from -0.2 to 4, as said below
- term_index: int32 [9, 2, 22], replicated, may hold values from 0 to 21, each once within a row
- term_value: float32 [9, 2, 22], replicated, may hold values from -1 to 1
Outputs:
- solution: float32 [44, 2048], P(('grp', 'chaos'), 'mesh'), parts along dimension 0
- residual: float32 [44, 2048], P(('grp', 'chaos'), 'mesh'), parts along dimension 0
There are 2 independent parts, one for each index of `grp`. A program takes and returns all parts, laid end to end along the dimension named above; an argument that names none is the same for every part. Nothing has to cross between parts.
Inputs may be any that keep to these rules, and one draw needn't show every extreme that they name: `halo_lists`: for every partition the 64 nodes of row 0 and the 64 nodes of row 1 are 128 different local nodes. `term_index`: for each random term and slot, the column modes over all row modes are a permutation of the modes. `coefficient`: row 0 lies in 1 to 4; each other row's entry is at most 0.05 times row 0's in magnitude.
All inputs are finite; a program needn't handle non-finite values.
Results may differ from a plain program's by a relative error of at most 0.0003.
Values sent between devices are 32-bit elements; how exact they have to be, the bound alone decides.
A program may use at most 128 MiB of HBM per device.

v0:
```python
import jax
import jax.numpy as jnp
from jax import lax
from jax.sharding import PartitionSpec as P

ITERS = 3


highest = lax.Precision.HIGHEST


def padded(block, sides, width):
    for axis, dim in sides:
        count = lax.axis_size(axis)
        forward = [(i, i + 1) for i in range(count - 1)]
        backward = [(target, source) for source, target in forward]
        low = lax.ppermute(
            lax.slice_in_dim(block, block.shape[dim] - width, None, axis=dim), axis, forward
        )
        high = lax.ppermute(lax.slice_in_dim(block, 0, width, axis=dim), axis, backward)
        block = jnp.concatenate([low, block, high], axis=dim)
    return block


def couple_terms(term_index, term_value):
    mode_count = term_index.shape[-1]
    columns = lax.broadcasted_iota(jnp.int32, term_index.shape + (mode_count,), 3)
    dense_table = jnp.sum(
        jnp.where(
            term_index[..., None] == columns, term_value[..., None], jnp.zeros((), term_value.dtype)
        ),
        axis=1,
    )
    mirror = 0.5 * (dense_table + jnp.swapaxes(dense_table, 1, 2))
    return jnp.concatenate([jnp.eye(mode_count, dtype=term_value.dtype)[None], mirror], axis=0)


def element_apply(extended, connect, gradients):
    picked = extended[:, connect]
    projected = jnp.einsum("dbe,rbe->rde", gradients, picked, precision=highest)
    return jnp.einsum("dae,rde->rae", gradients, projected, precision=highest)


def assemble(values, connect, weight, ext_width):
    row_count = values.shape[0]
    scaled = (values * weight[None, None, :]).reshape(row_count, -1)
    return jnp.zeros((row_count, ext_width), values.dtype).at[:, connect.reshape(-1)].add(scaled)


def extend(vector, down_list, up_list):
    halo_width = down_list.shape[0]
    outgoing = jnp.concatenate([vector[:, down_list], vector[:, up_list]], axis=1)
    widened = padded(outgoing, (("mesh", 1),), halo_width)
    return jnp.concatenate([vector, widened[:, :halo_width], widened[:, 3 * halo_width :]], axis=1)


def inner_pair(first, second, shared):
    return lax.psum((jnp.sum(first * shared), jnp.sum(second * shared)), ("mesh", "chaos"))


def per_device(
    right_side,
    preconditioner,
    mass_diag,
    halo_lists,
    connectivity,
    gradients,
    coefficient,
    term_index,
    term_value,
):
    coupling = couple_terms(term_index, term_value)
    term_count = coefficient.shape[0]
    mode_dev = right_side.shape[0]
    node_dev = right_side.shape[1]
    down_list = halo_lists[0]
    up_list = halo_lists[1]
    halo_width = down_list.shape[0]
    ext_width = node_dev + 2 * halo_width
    own_terms = lax.dynamic_slice_in_dim(coupling, lax.axis_index("kl") * term_count, term_count, 0)
    chaos_start = lax.axis_index("chaos") * mode_dev

    def operator(vector):
        extended = extend(vector, down_list, up_list)
        element_values = element_apply(extended, connectivity, gradients)
        stacked = jnp.concatenate(
            [
                assemble(element_values, connectivity, coefficient[term_id], ext_width)
                for term_id in range(term_count)
            ],
            axis=0,
        )
        columns = lax.dynamic_slice_in_dim(own_terms, chaos_start, mode_dev, 2)
        mixing = jnp.transpose(columns, (1, 0, 2)).reshape(columns.shape[1], term_count * mode_dev)
        groups = lax.axis_size("chaos")
        halves = lax.axis_size("kl")
        half_width = ext_width // halves
        blocks = jnp.einsum(
            "cim,mqh->cqih",
            mixing.reshape(groups, mode_dev, term_count * mode_dev),
            stacked.reshape(term_count * mode_dev, halves, half_width),
            precision=highest,
        )
        mine_half = lax.psum_scatter(
            blocks.reshape(groups * halves * mode_dev, half_width),
            ("chaos", "kl"),
            scatter_dimension=0,
            tiled=True,
        )
        summed = lax.all_gather(mine_half, "kl", axis=1, tiled=True)
        returned = padded(summed[:, node_dev:], (("mesh", 1),), halo_width)
        owned = (
            summed[:, :node_dev]
            .at[:, up_list]
            .add(returned[:, 3 * halo_width :])
            .at[:, down_list]
            .add(returned[:, :halo_width])
        )
        return owned + mass_diag[None, :] * vector

    solution = jnp.zeros_like(right_side)
    residual = right_side
    precond_res = preconditioner * residual
    image = operator(precond_res)
    dir_image = jnp.zeros_like(right_side)
    dir_precond = jnp.zeros_like(right_side)
    dir_residual = jnp.zeros_like(right_side)
    direction = jnp.zeros_like(right_side)
    gamma_old = None
    alpha_old = None
    for step_id in range(ITERS):
        gamma_now, delta_now = inner_pair(residual, image, precond_res)
        scaled_image = preconditioner * image
        product = operator(scaled_image)
        if step_id == 0:
            beta_now = jnp.zeros((), jnp.float32)
            alpha_now = gamma_now / delta_now
        else:
            beta_now = gamma_now / gamma_old
            alpha_now = gamma_now / (delta_now - beta_now * gamma_now / alpha_old)
        dir_image = product + beta_now * dir_image
        dir_precond = scaled_image + beta_now * dir_precond
        dir_residual = image + beta_now * dir_residual
        direction = precond_res + beta_now * direction
        solution = solution + alpha_now * direction
        residual = residual - alpha_now * dir_residual
        precond_res = precond_res - alpha_now * dir_precond
        image = image - alpha_now * dir_image
        gamma_old = gamma_now
        alpha_old = alpha_now
    return (solution, residual)


def solution(mesh):
    return jax.shard_map(
        per_device,
        mesh=mesh,
        in_specs=(
            P(("grp", "chaos"), "mesh"),
            P("chaos", "mesh"),
            P("mesh"),
            P(None, "mesh"),
            P(None, "mesh"),
            P(None, None, "mesh"),
            P(("grp", "kl"), "mesh"),
            P(),
            P(),
        ),
        out_specs=(P(("grp", "chaos"), "mesh"), P(("grp", "chaos"), "mesh")),
        check_vma=False,
    )
```

profile of v0, /device:TPU:0, one launch (start us, length us, event | category | flops | bytes accessed | tf_op | source)
XLA Modules:
  0.0 1395.8 jit_solution(11521515263827116520)
XLA Ops:
  24.6 34.2 %gather_fusion.2 = f32[10240,11]{1,0:T(8,128)} fusion(f32[11,640]{0,1:T(8,128)S(1)} %copy.249, s32[10240]{0:T(1024)S(1)} %broadcast_clamp_fusion), kind=kCustom, calls=%fused_computation.2 | custom fusion | bytes 942080 | tf_op jit(solution)/shard_map/gather | solution.py:39
  58.8 25.7 %fusion.13 = f32[2560,11,3]{1,2,0:T(4,128)S(1)} fusion(f32[3,4,2560]{1,0,2:T(4,128)} %copy.251, f32[4,2560,11]{2,1,0:T(8,128)} %bitcast.216), kind=kOutput, calls=%fused_computation.40 | convolution fusion | flops 4055040 | bytes 911360 | tf_op jit(solution)/shard_map/dbe,rbe->rde/dot_general | solution.py:40
  84.5 28.4 %multiply_bitcast_fusion.10 = (f32[11,4,2560]{0,1,2:T(4,128)}, f32[11,4,2560]{0,1,2:T(4,128)}, f32[11,4,2560]{0,1,2:T(4,128)}, f32[11,4,2560]{0,1,2:T(4,128)}, f32[11,4,2560]{0,1,2:T(4,128)}) fusion(f32[2560]{0:T(1024)S(1)} %get-tuple-element.12, f32[2560]{0:T(1024)S(1)} %get-tuple-element.16, f32[2560]{0:T(1024)S(1)} %get-tuple-element.13, ...), kind=kOutput, calls=%fused_computation.55 | convolution fusion | flops 4618240 | bytes 2764800 | tf_op jit(solution)/shard_map/dae,rde->rae/dot_general | solution.py:41
  120.3 55.6 %scatter_custom_fusion.1 = f32[11,640]{0,1:T(8,128)S(1)} fusion(s32[10240]{0:T(1024)S(1)} %bitcast.265, f32[10240,11]{1,0:T(8,128)} %copy.256, f32[]{:T(128)} %constant.34.clone.1), kind=kCustom, calls=%fused_computation.95 | custom fusion | flops 112640 | bytes 28672 | tf_op jit(solution)/shard_map/scatter-add | solution.py:47
  183.5 55.2 %scatter_custom_fusion.2 = f32[11,640]{0,1:T(8,128)S(1)} fusion(s32[10240]{0:T(1024)S(1)} %bitcast.266, f32[10240,11]{1,0:T(8,128)} %copy.258, f32[]{:T(128)} %constant.34.clone.1), kind=kCustom, calls=%fused_computation.93 | custom fusion | flops 112640 | bytes 28672 | tf_op jit(solution)/shard_map/scatter-add | solution.py:47
  246.4 55.2 %scatter_custom_fusion.3 = f32[11,640]{0,1:T(8,128)S(1)} fusion(s32[10240]{0:T(1024)S(1)} %bitcast.267, f32[10240,11]{1,0:T(8,128)} %copy.260, f32[]{:T(128)} %constant.34.clone.1), kind=kCustom, calls=%fused_computation.91 | custom fusion | flops 112640 | bytes 28672 | tf_op jit(solution)/shard_map/scatter-add | solution.py:47
  309.1 55.2 %scatter_custom_fusion.4 = f32[11,640]{0,1:T(8,128)S(1)} fusion(s32[10240]{0:T(1024)S(1)} %bitcast.268, f32[10240,11]{1,0:T(8,128)} %copy.262, f32[]{:T(128)} %constant.34.clone.1), kind=kCustom, calls=%fused_computation.89 | custom fusion | flops 112640 | bytes 28672 | tf_op jit(solution)/shard_map/scatter-add | solution.py:47
  372.0 55.2 %scatter_custom_fusion = f32[11,640]{0,1:T(8,128)S(1)} fusion(s32[10240]{0:T(1024)S(1)} %bitcast.269, f32[10240,11]{1,0:T(8,128)} %copy.254, f32[]{:T(128)} %constant.34.clone.1), kind=kCustom, calls=%fused_computation.97 | custom fusion | flops 112640 | bytes 28672 | tf_op jit(solution)/shard_map/scatter-add | solution.py:47
  464.6 34.4 %gather_fusion.5 = f32[10240,11]{1,0:T(8,128)} fusion(f32[11,640]{0,1:T(8,128)S(1)} %copy.286, s32[10240]{0:T(1024)S(1)} %broadcast_clamp_fusion), kind=kCustom, calls=%fused_computation.5 | custom fusion | bytes 942080 | tf_op jit(solution)/shard_map/gather | solution.py:39
  499.0 25.7 %fusion.9 = f32[2560,11,3]{1,2,0:T(4,128)S(1)} fusion(f32[3,4,2560]{1,0,2:T(4,128)} %copy.251, f32[4,2560,11]{2,1,0:T(8,128)} %bitcast.217), kind=kOutput, calls=%fused_computation.36 | convolution fusion | flops 4055040 | bytes 911360 | tf_op jit(solution)/shard_map/dbe,rbe->rde/dot_general | solution.py:40
  524.7 28.3 %multiply_bitcast_fusion.5 = (f32[11,4,2560]{0,1,2:T(4,128)}, f32[11,4,2560]{0,1,2:T(4,128)}, f32[11,4,2560]{0,1,2:T(4,128)}, f32[11,4,2560]{0,1,2:T(4,128)}, f32[11,4,2560]{0,1,2:T(4,128)}) fusion(f32[2560]{0:T(1024)S(1)} %get-tuple-element.12, f32[2560]{0:T(1024)S(1)} %get-tuple-element.16, f32[2560]{0:T(1024)S(1)} %get-tuple-element.13, ...), kind=kOutput, calls=%fused_computation.50 | convolution fusion | flops 4618240 | bytes 2764800 | tf_op jit(solution)/shard_map/dae,rde->rae/dot_general | solution.py:41
  560.4 55.6 %scatter_custom_fusion.8 = f32[11,640]{0,1:T(8,128)S(1)} fusion(s32[10240]{0:T(1024)S(1)} %bitcast.270, f32[10240,11]{1,0:T(8,128)} %copy.293, f32[]{:T(128)} %constant.34.clone.1), kind=kCustom, calls=%fused_computation.85 | custom fusion | flops 112640 | bytes 28672 | tf_op jit(solution)/shard_map/scatter-add | solution.py:47
  623.8 55.2 %scatter_custom_fusion.9 = f32[11,640]{0,1:T(8,128)S(1)} fusion(s32[10240]{0:T(1024)S(1)} %bitcast.271, f32[10240,11]{1,0:T(8,128)} %copy.295, f32[]{:T(128)} %constant.34.clone.1), kind=kCustom, calls=%fused_computation.83 | custom fusion | flops 112640 | bytes 28672 | tf_op jit(solution)/shard_map/scatter-add | solution.py:47
  686.6 55.2 %scatter_custom_fusion.10 = f32[11,640]{0,1:T(8,128)S(1)} fusion(s32[10240]{0:T(1024)S(1)} %bitcast.272, f32[10240,11]{1,0:T(8,128)} %copy.297, f32[]{:T(128)} %constant.34.clone.1), kind=kCustom, calls=%fused_computation.81 | custom fusion | flops 112640 | bytes 28672 | tf_op jit(solution)/shard_map/scatter-add | solution.py:47
  749.3 55.2 %scatter_custom_fusion.11 = f32[11,640]{0,1:T(8,128)S(1)} fusion(s32[10240]{0:T(1024)S(1)} %bitcast.273, f32[10240,11]{1,0:T(8,128)} %copy.299, f32[]{:T(128)} %constant.34.clone.1), kind=kCustom, calls=%fused_computation.79 | custom fusion | flops 112640 | bytes 28672 | tf_op jit(solution)/shard_map/scatter-add | solution.py:47
  812.2 55.2 %scatter_custom_fusion.7 = f32[11,640]{0,1:T(8,128)S(1)} fusion(s32[10240]{0:T(1024)S(1)} %bitcast.274, f32[10240,11]{1,0:T(8,128)} %copy.291, f32[]{:T(128)} %constant.34.clone.1), kind=kCustom, calls=%fused_computation.87 | custom fusion | flops 112640 | bytes 28672 | tf_op jit(solution)/shard_map/scatter-add | solution.py:47
  923.7 34.2 %gather_fusion.8 = f32[10240,11]{1,0:T(8,128)} fusion(f32[11,640]{0,1:T(8,128)S(1)} %copy.319, s32[10240]{0:T(1024)S(1)} %broadcast_clamp_fusion), kind=kCustom, calls=%fused_computation.8 | custom fusion | bytes 942080 | tf_op jit(solution)/shard_map/gather | solution.py:39
  957.9 25.7 %fusion.5 = f32[2560,11,3]{1,2,0:T(4,128)S(1)} fusion(f32[3,4,2560]{1,0,2:T(4,128)} %copy.251, f32[4,2560,11]{2,1,0:T(8,128)} %bitcast.215), kind=kOutput, calls=%fused_computation.32 | convolution fusion | flops 4055040 | bytes 911360 | tf_op jit(solution)/shard_map/dbe,rbe->rde/dot_general | solution.py:40
  983.6 28.4 %multiply_bitcast_fusion = (f32[11,4,2560]{0,1,2:T(4,128)}, f32[11,4,2560]{0,1,2:T(4,128)}, f32[11,4,2560]{0,1,2:T(4,128)}, f32[11,4,2560]{0,1,2:T(4,128)}, f32[11,4,2560]{0,1,2:T(4,128)}) fusion(f32[2560]{0:T(1024)S(1)} %get-tuple-element.12, f32[2560]{0:T(1024)S(1)} %get-tuple-element.16, f32[2560]{0:T(1024)S(1)} %get-tuple-element.13, ...), kind=kOutput, calls=%fused_computation.45 | convolution fusion | flops 4618240 | bytes 2764800 | tf_op jit(solution)/shard_map/dae,rde->rae/dot_general | solution.py:41
  1019.4 55.4 %scatter_custom_fusion.15 = f32[11,640]{0,1:T(8,128)S(1)} fusion(s32[10240]{0:T(1024)S(1)} %bitcast.275, f32[10240,11]{1,0:T(8,128)} %copy.326, f32[]{:T(128)} %constant.34.clone.1), kind=kCustom, calls=%fused_computation.75 | custom fusion | flops 112640 | bytes 28672 | tf_op jit(solution)/shard_map/scatter-add | solution.py:47
  1082.4 55.2 %scatter_custom_fusion.16 = f32[11,640]{0,1:T(8,128)S(1)} fusion(s32[10240]{0:T(1024)S(1)} %bitcast.276, f32[10240,11]{1,0:T(8,128)} %copy.328, f32[]{:T(128)} %constant.34.clone.1), kind=kCustom, calls=%fused_computation.73 | custom fusion | flops 112640 | bytes 28672 | tf_op jit(solution)/shard_map/scatter-add | solution.py:47
  1145.3 55.2 %scatter_custom_fusion.17 = f32[11,640]{0,1:T(8,128)S(1)} fusion(s32[10240]{0:T(1024)S(1)} %bitcast.277, f32[10240,11]{1,0:T(8,128)} %copy.330, f32[]{:T(128)} %constant.34.clone.1), kind=kCustom, calls=%fused_computation.71 | custom fusion | flops 112640 | bytes 28672 | tf_op jit(solution)/shard_map/scatter-add | solution.py:47
  1208.1 55.2 %scatter_custom_fusion.18 = f32[11,640]{0,1:T(8,128)S(1)} fusion(s32[10240]{0:T(1024)S(1)} %bitcast.278, f32[10240,11]{1,0:T(8,128)} %copy.332, f32[]{:T(128)} %constant.34.clone.1), kind=kCustom, calls=%fused_computation.69 | custom fusion | flops 112640 | bytes 28672 | tf_op jit(solution)/shard_map/scatter-add | solution.py:47
  1270.9 55.5 %scatter_custom_fusion.14 = f32[11,640]{0,1:T(8,128)S(1)} fusion(s32[10240]{0:T(1024)S(1)} %bitcast.279, f32[10240,11]{1,0:T(8,128)} %copy.324, f32[]{:T(128)} %constant.34.clone.1), kind=kCustom, calls=%fused_computation.77 | custom fusion | flops 112640 | bytes 28672 | tf_op jit(solution)/shard_map/scatter-add | solution.py:47
  (241 shorter events, 288.2 us)
Async XLA Ops:
  3.0 21.3 %collective-permute-start = (f32[11,64]{1,0:T(8,128)S(1)}, f32[11,64]{1,0:T(8,128)S(1)}, u32[]{:S(2)}, u32[]{:S(2)}) collective-permute-start(f32[11,64]{1,0:T(8,128)S(1)} %bitcast.280), channel_id=1, source_target_pairs={{0,4},{4,8},{8,12},{1,5},{5,9},{9,13},{2,6},{6,10},{10,14},{3,7},{... | collective-permute-start | bytes 8456 | tf_op jit(solution)/shard_map/ppermute | solution.py:17
  8.6 15.7 %collective-permute-start.1 = (f32[11,64]{1,0:T(8,128)S(1)}, f32[11,64]{1,0:T(8,128)S(1)}, u32[]{:S(2)}, u32[]{:S(2)}) collective-permute-start(f32[11,64]{1,0:T(8,128)S(1)} %bitcast.281), channel_id=1, source_target_pairs={{4,0},{8,4},{12,8},{5,1},{9,5},{13,9},{6,2},{10,6},{14,10},{7,3},{... | collective-permute-start | bytes 8456 | tf_op jit(solution)/shard_map/ppermute | solution.py:20
  24.6 59.9 %slice-start = ((s8[5242880]{0:T(1024)(128)(4,1)}), s8[1048576]{0:T(1024)(128)(4,1)S(1)}, s32[]{:S(2)}) async-start(s8[5242880]{0:T(1024)(128)(4,1)} %bitcast.218), calls=%async_computation | async-start | bytes 2097152
  368.5 69.2 %copy-start.4 = (u32[32]{0:T(128)S(1)}, u32[32]{0:T(128)}, u32[]{:S(2)}) copy-start(u32[32]{0:T(128)} %constant.49) | copy-start | bytes 388
  368.5 80.4 %copy-start.3 = (f32[512]{0:T(512)S(1)}, f32[512]{0:T(512)}, u32[]{:S(2)}) copy-start(f32[512]{0:T(512)} %param.11) | copy-start | bytes 6148
  368.6 83.9 %copy-start.1 = (f32[11,512]{1,0:T(8,128)S(1)}, f32[11,512]{1,0:T(8,128)}, u32[]{:S(2)}) copy-start(f32[11,512]{1,0:T(8,128)} %param.9) | copy-start | bytes 67588
  368.6 83.9 %copy-start.2 = (f32[11,512]{1,0:T(8,128)S(1)}, f32[11,512]{1,0:T(8,128)}, u32[]{:S(2)}) copy-start(f32[11,512]{1,0:T(8,128)} %param.10) | copy-start | bytes 67588
  436.3 2.6 collective-permute-start.12
  442.6 6.4 collective-permute-start.2
  443.9 6.3 collective-permute-start.3
  454.5 5.6 collective-permute-start.4
  458.8 5.5 collective-permute-start.5
  464.6 60.1 %slice-start.2 = ((s8[5242880]{0:T(1024)(128)(4,1)}), s8[1048576]{0:T(1024)(128)(4,1)S(1)}, s32[]{:S(2)}) async-start(s8[5242880]{0:T(1024)(128)(4,1)} %bitcast.220), calls=%async_computation.2 | async-start | bytes 2097152
  499.0 25.7 %slice-start.3 = ((s8[5242880]{0:T(1024)(128)(4,1)}), s8[4194304]{0:T(1024)(128)(4,1)S(1)}, s32[]{:S(2)}) async-start(s8[5242880]{0:T(1024)(128)(4,1)} %bitcast.220), calls=%async_computation.3 | async-start | bytes 8388608
  876.9 22.9 %collective-permute-start.13 = (f32[15,320]{1,0:T(8,128)S(1)}, f32[15,320]{1,0:T(8,128)S(1)}, u32[]{:S(2)}, u32[]{:S(2)}) collective-permute-start(f32[15,320]{1,0:T(8,128)S(1)} %slice.111), channel_id=1, source_target_pairs={{0,1},{1,2},{2,3},{4,5},{5,6},{6,7},{8,9},{9,10},{10,11},{12,13},{... | collective-permute-start | bytes 57608
  902.0 6.0 collective-permute-start.6
  903.3 5.9 collective-permute-start.7
  913.6 5.7 collective-permute-start.8
  917.9 5.5 collective-permute-start.9
  923.7 59.9 %slice-start.4 = ((s8[5242880]{0:T(1024)(128)(4,1)}), s8[1048576]{0:T(1024)(128)(4,1)S(1)}, s32[]{:S(2)}) async-start(s8[5242880]{0:T(1024)(128)(4,1)} %bitcast.222), calls=%async_computation.4 | async-start | bytes 2097152
  957.9 25.7 %slice-start.5 = ((s8[5242880]{0:T(1024)(128)(4,1)}), s8[4194304]{0:T(1024)(128)(4,1)S(1)}, s32[]{:S(2)}) async-start(s8[5242880]{0:T(1024)(128)(4,1)} %bitcast.222), calls=%async_computation.5 | async-start | bytes 8388608
  1334.0 25.8 %collective-permute-start.14 = (f32[15,320]{1,0:T(8,128)S(1)}, f32[15,320]{1,0:T(8,128)S(1)}, u32[]{:S(2)}, u32[]{:S(2)}) collective-permute-start(f32[15,320]{1,0:T(8,128)S(1)} %slice.112), channel_id=1, source_target_pairs={{0,1},{1,2},{2,3},{4,5},{5,6},{6,7},{8,9},{9,10},{10,11},{12,13},{... | collective-permute-start | bytes 57608
  1362.1 6.0 collective-permute-start.10
  1363.3 5.9 collective-permute-start.11
  (2 other events, 45.7 us)
where the time goes:
time: 1410 us; the launch traced here: 1400 us
  other arithmetic  843 us (60%)
  local copies, waits for them, and re-layouts  239 us (17%)
  matrix products  163 us (12%)
  blocking collectives  87.5 us (6%)
  starting transfers between devices  39.3 us (3%)
    scatter-add x15, other arithmetic, assemble(): jnp.zeros((row_count, ext_width), values.dtype).at[:, connect.reshape(-1)]  830 us
    gather x3, local copies, waits for them, and re-layouts, element_apply(): picked = extended[:, connect]  103 us
    dot_general x3, matrix products, element_apply(): return jnp.einsum('dae,rde->rae', gradients, projected, precision=highest)  85.1 us
    dot_general x3, matrix products, element_apply(): projected = jnp.einsum('dbe,rbe->rde', gradients, picked, precision=highest)  77 us
    mul x15, local copies, waits for them, and re-layouts, assemble(): scaled = (values * weight[None, None, :]).reshape(row_count, -1)  59.7 us
    psum x3, blocking collectives, inner_pair(): lax.psum((jnp.sum(first * shared), jnp.sum(second * shared)), ('mesh', 'c...  57.8 us
    reshape x15, local copies, waits for them, and re-layouts, assemble(): scaled = (values * weight[None, None, :]).reshape(row_count, -1)  47.4 us
  transfers between devices with their start and end apart: 15, of which 5 were waited for; matrix products, arithmetic and copies ran while one was open for 1% of the time, Pallas kernels for 0%

commit v1 on v0

v1 whole, which is shorter than its diff:
```python
import functools

import jax
import jax.numpy as jnp
from jax import lax
from jax.experimental import pallas as pl
from jax.experimental.pallas import tpu as pltpu
from jax.sharding import PartitionSpec as P

ITERS = 3
OPS = ITERS
F32 = jnp.float32
BF16 = jnp.bfloat16
MESH = pl.DeviceIdType.MESH


def round_up(value, unit):
    return -(-value // unit) * unit


def split(value, parts):
    pieces = []
    rest = value
    for _ in range(parts - 1):
        high = rest.astype(BF16).astype(F32)
        pieces.append(high)
        rest = rest - high
    pieces.append(rest)
    return jnp.concatenate(pieces, axis=0).astype(BF16)


def fold(value, rows):
    total = value[:rows]
    for start in range(rows, value.shape[0], rows):
        total = total + value[start : start + rows]
    return total


def dot(left, right):
    return lax.dot_general(left, right, (((1,), (0,)), ((), ())), preferred_element_type=F32)


def dot_t(left, right):
    return lax.dot_general(left, right, (((1,), (1,)), ((), ())), preferred_element_type=F32)


def kernel(
    dims,
    rhs_in,
    pre_in,
    mass_in,
    halo_in,
    conn_in,
    grad_in,
    coef_in,
    mix_in,
    x_out,
    res_out,
    gathered,
    coefs,
    dstack,
    dsend,
    zinit,
    ids,
    oht,
    halo_oh,
    base,
    mass_ext,
    mix,
    sc_hi,
    sc_lo,
    loc,
    part,
    from_x,
    from_z,
    dot_send,
    dot_recv,
    sem_gs,
    sem_gr,
    sem_cs,
    sem_cr,
    sem_zis,
    sem_zir,
    sem_xs,
    sem_xr,
    sem_zs,
    sem_zr,
    sem_ds,
    sem_dr,
):
    n_mesh, n_chaos, n_kl, modes, mode_dev, node, halo, elems, chunk, terms, term_dev = dims
    rows = round_up(modes, 8)
    rd = round_up(mode_dev, 8)
    pairs = round_up(terms, 2)
    wide = node + 4 * halo
    low_at, up_at = node, node + 2 * halo

    m = lax.axis_index("mesh")
    c = lax.axis_index("chaos")
    k = lax.axis_index("kl")
    has_low = m > 0
    has_up = m < n_mesh - 1
    sides = ((0, has_low, m - 1), (1, has_up, m + 1))

    def peer_c(off):
        return lax.rem(c + off, n_chaos)

    def source_c(off):
        return lax.rem(c + n_chaos - off, n_chaos)

    barrier = pltpu.get_barrier_semaphore()

    def greet(target):
        pl.semaphore_signal(barrier, inc=1, device_id=target, device_id_type=MESH)

    for off in range(1, n_chaos):
        greet({"chaos": peer_c(off)})
    for off in range(1, n_mesh):
        greet({"mesh": lax.rem(m + off, n_mesh)})
    for off in range(1, n_kl):
        greet({"kl": lax.rem(k + off, n_kl)})
    for _, has, other in sides:
        @pl.when(has)
        def _():
            for off in range(1, n_chaos):
                greet({"mesh": other, "chaos": peer_c(off)})

    neighbours = jnp.where(has_low, 1, 0) + jnp.where(has_up, 1, 0)
    pl.semaphore_wait(
        barrier, n_chaos - 1 + n_mesh - 1 + n_kl - 1 + neighbours * (n_chaos - 1)
    )

    def remote(src, dst, send, recv, target):
        return pltpu.make_async_remote_copy(
            src_ref=src, dst_ref=dst, send_sem=send, recv_sem=recv,
            device_id=target, device_id_type=MESH,
        )

    elem_at = pl.multiple_of(c * elems, 128)
    mine = pl.ds(elem_at, elems)
    pending = []

    coef_waits = []
    for off in range(1, n_kl):
        copy = remote(
            coef_in.at[:, mine], coefs.at[k], sem_cs.at[off], sem_cr.at[off],
            {"kl": lax.rem(k + off, n_kl)},
        )
        copy.start()
        pending.append((None, copy))
        source = lax.rem(k + n_kl - off, n_kl)
        coef_waits.append(
            remote(coef_in.at[:, mine], coefs.at[source], sem_cs.at[off], sem_cr.at[off],
                   {"kl": lax.rem(k + off, n_kl)})
        )
    gather_waits = []
    for off in range(1, n_chaos):
        for which, ref in enumerate((rhs_in, pre_in)):
            target = {"chaos": peer_c(off)}
            sems = (sem_gs.at[off, which], sem_gr.at[off, which])
            copy = remote(ref, gathered.at[which, c], *sems, target)
            copy.start()
            pending.append((None, copy))
            gather_waits.append(remote(ref, gathered.at[which, source_c(off)], *sems, target))
    coefs[k] = coef_in[:, mine]
    gathered[0, c] = rhs_in[...]
    gathered[1, c] = pre_in[...]

    hrow = jnp.concatenate([halo_in[0:1, :], halo_in[1:2, :]], axis=1)
    sub = lax.broadcasted_iota(jnp.int32, (node, 2 * halo), 0)
    hits = jnp.where(sub == hrow, 1.0, 0.0).astype(F32)
    halo_oh[...] = hits.astype(BF16)
    in_halo = jnp.sum(hits, axis=1, keepdims=True)

    dstack[...] = jnp.zeros_like(dstack)
    dstack[0:mode_dev, :] = rhs_in[...]
    dstack[rd : rd + mode_dev, :] = pre_in[...]
    dstack[2 * rd : 2 * rd + 1, :] = mass_in[...]
    dsend[...] = fold(dot(split(dstack[...], 3), halo_oh[...]), dsend.shape[0])

    def to_sides(source_of, dst_of, send_of, recv_of):
        copies = []
        for side, has, other in sides:
            for off in range(n_chaos):
                copy = remote(
                    source_of(side), dst_of(1 - side, off),
                    send_of(side, off), recv_of(1 - side, off),
                    {"mesh": other, "chaos": peer_c(off)},
                )
                arrival = remote(
                    source_of(side), dst_of(side, off),
                    send_of(side, off), recv_of(side, off),
                    {"mesh": other, "chaos": peer_c(off)},
                )
                pl.when(has)(copy.start)
                pending.append((has, copy))
                copies.append((has, arrival))
        return copies

    zinit_waits = []
    for side, has, other in sides:
        for off in range(n_chaos):
            target = {"mesh": other, "chaos": peer_c(off)}
            copy = remote(dsend, zinit.at[1 - side, c], sem_zis.at[side, off],
                          sem_zir.at[1 - side, off], target)
            pl.when(has)(copy.start)
            pending.append((has, copy))
            zinit_waits.append(
                (has, remote(dsend, zinit.at[side, source_c(off)], sem_zis.at[side, off],
                             sem_zir.at[side, off], target))
            )

    square = 2 * halo
    spread = jnp.broadcast_to(hrow.astype(F32), (square, square))
    columns = jnp.transpose(spread).astype(jnp.int32)
    ids[0:node, :] = jnp.where(in_halo > 0.0, -1, sub)
    ghost = lax.broadcasted_iota(jnp.int32, (halo, square), 0) + node
    ids[low_at : low_at + halo, :] = ghost
    ids[low_at + halo : up_at, :] = columns[:halo]
    ids[up_at : up_at + halo, :] = ghost + halo
    ids[up_at + halo : wide, :] = columns[halo:]

    for corner in range(4):
        for tile in range(elems // 128):
            slots = conn_in[corner : corner + 1, pl.ds(elem_at + tile * 128, 128)]
            at = corner * elems + tile * 128
            oht[:, at : at + 128] = jnp.where(ids[...] == slots, 1.0, 0.0).astype(BF16)

    mix[...] = split(mix_in[...], 2)
    for buffer in range(2):
        if pairs > terms:
            sc_hi[buffer] = jnp.zeros_like(sc_hi[buffer])
            sc_lo[buffer] = jnp.zeros_like(sc_lo[buffer])

    for copy in coef_waits:
        copy.wait_recv()
    for copy in gather_waits:
        copy.wait_recv()
    for has, copy in zinit_waits:
        pl.when(has)(copy.wait_recv)

    lane = lax.broadcasted_iota(jnp.int32, (1, square), 1)
    first_half = lane < halo
    own_col = jnp.transpose(jnp.broadcast_to(in_halo, (node, 128)))[0:1]
    keep = jnp.where(own_col > 0.0, 0.0, 1.0)

    def blocks(dup, low, up):
        low = jnp.where(has_low, low, 0.0)
        up = jnp.where(has_up, up, 0.0)
        return (
            pltpu.roll(jnp.where(first_half, dup, low), halo, 1),
            jnp.where(first_half, up, dup),
        )

    base[...] = jnp.zeros_like(base)
    for which in range(2):
        for group in range(n_chaos):
            at = slice(group * mode_dev, (group + 1) * mode_dev)
            base[which, at, 0:node] = gathered[which, group]
            base[which, at, low_at:up_at] = zinit[0, group, which * rd : which * rd + mode_dev]
            base[which, at, up_at:wide] = zinit[1, group, which * rd : which * rd + mode_dev]
    for which in range(2):
        own = base[which, :, 0:node]
        dup = fold(dot(split(own, 3), halo_oh[...]), rows)
        low, up = blocks(dup, base[which, :, low_at:up_at], base[which, :, up_at:wide])
        base[which, :, 0:node] = own * keep
        base[which, :, low_at:up_at] = low
        base[which, :, up_at:wide] = up
    mass_dup = dsend[2 * rd : 2 * rd + 1, :]
    low, up = blocks(
        mass_dup, zinit[0, 0, 2 * rd : 2 * rd + 1, :], zinit[1, 0, 2 * rd : 2 * rd + 1, :]
    )
    mass_ext[:, 0:node] = mass_in[...]
    mass_ext[:, low_at:up_at] = low
    mass_ext[:, up_at:wide] = up

    lanes = lax.broadcasted_iota(jnp.int32, (1, wide), 1)
    counted = (lanes < node) | (lax.rem(lanes // halo, 2) == 1)
    counted = jnp.where(counted, 1.0, 0.0).astype(F32)

    def apply_local(vector, op):
        stacked = split(vector, 2)
        for step in range(elems // chunk):
            at = step * chunk
            here = pl.ds(elem_at + at, chunk)
            corners = [
                fold(dot(stacked, oht[:, b * elems + at : b * elems + at + chunk]), rows)
                for b in range(4)
            ]
            buffer = step % 2
            main = []
            for d in range(3):
                projected = grad_in[d, 0:1, here] * corners[0]
                for b in range(1, 4):
                    projected = projected + grad_in[d, b : b + 1, here] * corners[b]
                main.append(coefs[0, 0:1, at : at + chunk] * projected)
                for first in range(1, terms + 1, 2):
                    pair = []
                    for term in range(first, min(first + 2, terms + 1)):
                        group, entry = divmod(term, term_dev)
                        pair.append(coefs[group, entry : entry + 1, at : at + chunk] * projected)
                    while len(pair) < 2:
                        pair.append(jnp.zeros_like(projected))
                    both = jnp.concatenate(pair, axis=0)
                    high = both.astype(BF16)
                    to = slice((first - 1) * rows, (first + 1) * rows)
                    sc_hi[buffer, to, d * chunk : (d + 1) * chunk] = high
                    sc_lo[buffer, to, d * chunk : (d + 1) * chunk] = (
                        both - high.astype(F32)
                    ).astype(BF16)
            mixed = fold(dot(mix[...], sc_hi[buffer]), rows)
            mixed = mixed + dot(mix[...], sc_lo[buffer])[:rows]
            for a in range(4):
                local = None
                for d in range(3):
                    piece = grad_in[d, a : a + 1, here] * (
                        main[d] + mixed[:, d * chunk : (d + 1) * chunk]
                    )
                    local = piece if local is None else local + piece
                loc[:, a * elems + at : a * elems + at + chunk] = split(local, 2)
        part[op] = fold(dot_t(loc[...], oht[...]), rows)

    def send_parts(op):
        arrivals = []
        for off in range(1, n_chaos):
            copy = remote(part.at[op], from_x.at[op, off], sem_xs.at[op, off],
                          sem_xr.at[op, off], {"chaos": peer_c(off)})
            copy.start()
            pending.append((None, copy))
            arrivals.append((None, copy))
        spans = (slice(low_at, up_at), slice(up_at, wide))
        arrivals += to_sides(
            lambda side: part.at[op, :, spans[side]],
            lambda side, off: from_z.at[op, side, off],
            lambda side, off: sem_zs.at[op, side, off],
            lambda side, off: sem_zr.at[op, side, off],
        )
        return arrivals

    def finish(vector, op, arrivals):
        for has, copy in arrivals:
            if has is None:
                copy.wait_recv()
            else:
                pl.when(has)(copy.wait_recv)
        total = part[op]
        for off in range(1, n_chaos):
            total = total + from_x[op, off]
        edges = []
        for side, has, _ in sides:
            edge = from_z[op, side, 0]
            for off in range(1, n_chaos):
                edge = edge + from_z[op, side, off]
            edges.append(pltpu.roll(jnp.where(has, edge, 0.0), halo, 1))
        total = total + jnp.concatenate([jnp.zeros((rows, node), F32)] + edges, axis=1)
        return total + mass_ext[...] * vector

    def tile_sum(first, second):
        product = first * second * counted
        total = None
        for row in range(0, rows, 8):
            for at in range(0, wide, 128):
                piece = product[row : row + 8, at : at + 128]
                total = piece if total is None else total + piece
        return total

    def send_dots(step, residual, image, shared):
        dot_send[step, 0] = tile_sum(residual, shared)
        dot_send[step, 1] = tile_sum(image, shared)
        dot_recv[step, m] = dot_send[step]
        arrivals = []
        for off in range(1, n_mesh):
            target = {"mesh": lax.rem(m + off, n_mesh)}
            sems = (sem_ds.at[step, off], sem_dr.at[step, off])
            copy = remote(dot_send.at[step], dot_recv.at[step, m], *sems, target)
            copy.start()
            pending.append((None, copy))
            source = lax.rem(m + n_mesh - off, n_mesh)
            arrivals.append(remote(dot_send.at[step], dot_recv.at[step, source], *sems, target))
        return arrivals

    def take_dots(step, arrivals):
        for copy in arrivals:
            copy.wait_recv()
        total = dot_recv[step, 0]
        for source in range(1, n_mesh):
            total = total + dot_recv[step, source]
        sums = [
            jnp.sum(jnp.sum(total[i], axis=0, keepdims=True), axis=1, keepdims=True)
            for i in range(2)
        ]
        return sums

    residual = base[0]
    pre = base[1]
    shared = pre * residual
    apply_local(shared, 0)
    image = finish(shared, 0, send_parts(0))
    dir_image = dir_pre = dir_res = direction = None
    answer = None
    gamma_old = alpha_old = None
    for step in range(ITERS):
        dots = send_dots(step, residual, image, shared)
        last = step == ITERS - 1
        scaled = pre * image
        if not last:
            apply_local(scaled, step + 1)
            arrivals = send_parts(step + 1)
        gamma, delta = take_dots(step, dots)
        if step == 0:
            alpha = gamma / delta
            dir_pre, dir_res, direction = scaled, image, shared
            answer = alpha * direction
        else:
            beta = gamma / gamma_old
            alpha = gamma / (delta - beta * gamma / alpha_old)
            dir_pre = scaled + beta * dir_pre
            dir_res = image + beta * dir_res
            direction = shared + beta * direction
            answer = answer + alpha * direction
        residual = residual - alpha * dir_res
        shared = shared - alpha * dir_pre
        if not last:
            product = finish(scaled, step + 1, arrivals)
            dir_image = product if step == 0 else product + beta * dir_image
            image = image - alpha * dir_image
        gamma_old, alpha_old = gamma, alpha

    for out, value in ((x_out, answer), (res_out, residual)):
        dup = jnp.where(
            first_half, pltpu.roll(value[:, low_at:up_at], halo, 1), value[:, up_at:wide]
        )
        own = value[:, :node] + fold(dot_t(split(dup, 3), halo_oh[...]), rows)
        base[0, :, 0:node] = own
        for group in range(n_chaos):
            @pl.when(c == group)
            def _():
                out[...] = base[0, group * mode_dev : (group + 1) * mode_dev, 0:node]

    for has, copy in pending:
        if has is None:
            copy.wait_send()
        else:
            pl.when(has)(copy.wait_send)


def couple_terms(term_index, term_value, rows, pairs):
    mode_count = term_index.shape[-1]
    columns = lax.broadcasted_iota(jnp.int32, term_index.shape + (mode_count,), 3)
    table = jnp.sum(
        jnp.where(term_index[..., None] == columns, term_value[..., None], 0.0), axis=1
    )
    mirror = 0.5 * (table + jnp.swapaxes(table, 1, 2))
    pad = rows - mode_count
    mirror = jnp.pad(mirror, ((0, pairs - mirror.shape[0]), (0, pad), (0, pad)))
    return jnp.transpose(mirror, (1, 0, 2)).reshape(rows, pairs * rows)


def per_device(
    right_side,
    preconditioner,
    mass_diag,
    halo_lists,
    connectivity,
    gradients,
    coefficient,
    term_index,
    term_value,
):
    n_mesh, n_chaos, n_kl = (lax.axis_size(axis) for axis in ("mesh", "chaos", "kl"))
    mode_dev, node = right_side.shape
    modes = mode_dev * n_chaos
    halo = halo_lists.shape[1]
    elem_dev = connectivity.shape[1]
    term_dev = coefficient.shape[0]
    terms = term_dev * n_kl - 1
    rows, rd, pairs = round_up(modes, 8), round_up(mode_dev, 8), round_up(terms, 2)
    elems = round_up(-(-elem_dev // n_chaos), 128)
    chunk = 256 if elems % 256 == 0 else 128
    wide = node + 4 * halo
    extra = elems * n_chaos - elem_dev
    if extra:
        connectivity = jnp.pad(connectivity, ((0, 0), (0, extra)))
        gradients = jnp.pad(gradients, ((0, 0), (0, 0), (0, extra)))
        coefficient = jnp.pad(coefficient, ((0, 0), (0, extra)))
    mix = couple_terms(term_index, term_value, rows, pairs)
    dims = (n_mesh, n_chaos, n_kl, modes, mode_dev, node, halo, elems, chunk, terms, term_dev)
    vmem = pltpu.VMEM
    dma = pltpu.SemaphoreType.DMA
    drows = 2 * rd + 8
    return pl.pallas_call(
        functools.partial(kernel, dims),
        out_shape=[jax.ShapeDtypeStruct((mode_dev, node), F32)] * 2,
        in_specs=[pl.BlockSpec(memory_space=vmem)] * 8,
        out_specs=[pl.BlockSpec(memory_space=vmem)] * 2,
        scratch_shapes=[
            vmem((2, n_chaos, mode_dev, node), F32),
            vmem((n_kl, term_dev, elems), F32),
            vmem((drows, node), F32),
            vmem((drows, 2 * halo), F32),
            vmem((2, n_chaos, drows, 2 * halo), F32),
            vmem((wide, 2 * halo), jnp.int32),
            vmem((wide, 4 * elems), BF16),
            vmem((node, 2 * halo), BF16),
            vmem((2, rows, wide), F32),
            vmem((1, wide), F32),
            vmem((2 * rows, pairs * rows), BF16),
            vmem((2, pairs * rows, 3 * chunk), BF16),
            vmem((2, pairs * rows, 3 * chunk), BF16),
            vmem((2 * rows, 4 * elems), BF16),
            vmem((OPS, rows, wide), F32),
            vmem((OPS, n_chaos, rows, wide), F32),
            vmem((OPS, 2, n_chaos, rows, 2 * halo), F32),
            vmem((ITERS, 2, 8, 128), F32),
            vmem((ITERS, n_mesh, 2, 8, 128), F32),
            dma((n_chaos, 2)),
            dma((n_chaos, 2)),
            dma((n_kl,)),
            dma((n_kl,)),
            dma((2, n_chaos)),
            dma((2, n_chaos)),
            dma((OPS, n_chaos)),
            dma((OPS, n_chaos)),
            dma((OPS, 2, n_chaos)),
            dma((OPS, 2, n_chaos)),
            dma((ITERS, n_mesh)),
            dma((ITERS, n_mesh)),
        ],
        compiler_params=pltpu.CompilerParams(
            collective_id=0, has_side_effects=True, vmem_limit_bytes=56 * 2**20
        ),
    )(
        right_side,
        preconditioner,
        mass_diag.reshape(1, node),
        halo_lists,
        connectivity,
        gradients,
        coefficient,
        mix,
    )


def solution(mesh):
    return jax.shard_map(
        per_device,
        mesh=mesh,
        in_specs=(
            P(("grp", "chaos"), "mesh"),
            P("chaos", "mesh"),
            P("mesh"),
            P(None, "mesh"),
            P(None, "mesh"),
            P(None, None, "mesh"),
            P(("grp", "kl"), "mesh"),
            P(),
            P(),
        ),
        out_specs=(P(("grp", "chaos"), "mesh"), P(("grp", "chaos"), "mesh")),
        check_vma=False,
    )
```

time: 1410 us -> 50.3 us (0.04)
  other arithmetic: 843 us -> 1.18 us
  local copies, waits for them, and re-layouts: 239 us -> 3.9 us
  matrix products: 163 us -> 0 us
  blocking collectives: 87.5 us -> 0 us
  Pallas kernels: 0 us -> 44.3 us
  starting transfers between devices: 39.3 us -> 0 us
    scatter-add x21 -> x0, other arithmetic: 836 us -> none  [the longest x15 830 us: assemble(): jnp.zeros((row_count, ext_width), values.dtype).at[:, connect.reshape(-1)]]
    dot_general x9 -> x0, matrix products: 163 us -> none  [the longest x3 85.1 us: element_apply(): return jnp.einsum('dae,rde->rae', gradients, projected, precision=highest)]
    gather x15 -> x0, local copies, waits for them, and re-layouts: 107 us -> none  [the longest x3 103 us: element_apply(): picked = extended[:, connect]]
    mul x18 -> x0, local copies, waits for them, and re-layouts: 60.1 us -> none  [the longest x15 59.7 us: assemble(): scaled = (values * weight[None, None, :]).reshape(row_count, -1)]
    psum x3 -> x0, blocking collectives: 57.8 us -> none  [inner_pair(): lax.psum((jnp.sum(first * shared), jnp.sum(second * shared)), ('mesh', 'c...]
    reshape x21 -> x1, local copies, waits for them, and re-layouts: 47.9 us -> 0.71 us  [couple_terms(): return jnp.transpose(mirror, (1, 0, 2)).reshape(rows, pairs * rows)]
    pallas_call x0 -> x1, Pallas kernels: none -> 44.3 us  [per_device(): pl.pallas_call(functools.partial(kernel, dims), out_shape=[jax.ShapeDtype...]
    ppermute x12 -> x0, starting transfers between devices: 35.2 us -> none  [the longest x6 27.3 us: padded(): lax.ppermute(lax.slice_in_dim(block, block.shape[dim] - width, None, axis...]
  transfers between devices with their start and end apart: 15 -> 0, of which waited for: 5 -> 0; matrix products, arithmetic and copies ran while one was open for 1% -> 0% of each run, Pallas kernels for 0% -> 0%
where the time goes in v1:
time: 50.3 us; the launch traced here: 50.1 us
  Pallas kernels  44.3 us (88%)
  local copies, waits for them, and re-layouts  3.9 us (8%)
  other arithmetic  1.18 us (2%)
  between operations  0.68 us (1%)
    pallas_call x1, Pallas kernels, per_device(): pl.pallas_call(functools.partial(kernel, dims), out_shape=[jax.ShapeDtype...  44.3 us
    unnamed x8, local copies, waits for them, and re-layouts  3 us
    reduce_sum x1, other arithmetic, couple_terms(): jnp.sum(jnp.where(term_index[..., None] == columns, term_value[..., None]...  1.16 us

profile of v1, /device:TPU:0, one launch (start us, length us, event | category | flops | bytes accessed | tf_op | source)
XLA Modules:
  0.0 50.1 jit_solution(11788943954317532832)
XLA Ops:
  0.6 0.0 copy-start.1
  0.6 0.8 %copy.13 = s32[9,2,22]{1,2,0:T(8,128)S(1)} copy(s32[9,2,22]{2,1,0:T(2,128)} %param.16) | data formatting | bytes 3168 | tf_op args[7]
  1.5 0.0 copy-done.1
  1.5 0.1 copy.14
  1.6 1.2 %fusion = f32[9,22,22]{2,1,0:T(8,128)S(1)} fusion(f32[9,2,22]{1,2,0:T(8,128)S(1)} %copy.14, s32[9,2,22]{1,2,0:T(8,128)S(1)} %copy.13), kind=kLoop, calls=%fused_computation.1 | loop fusion | flops 21780 | bytes 20592 | tf_op jit(solution)/shard_map/reduce_sum | solution.py:450
  2.8 0.1 copy.15
  3.0 0.7 %reshape.13.mix_in = f32[24,240]{1,0:T(8,128)} reshape(f32[24,10,24]{2,1,0:T(8,128)S(1)} %copy.16) | data formatting | bytes 46080 | tf_op jit(solution)/shard_map/reshape | solution.py:456
  3.7 44.3 %shard_map.104 = (f32[11,512]{1,0:T(8,128)}, f32[11,512]{1,0:T(8,128)}) custom-call(f32[11,512]{1,0:T(8,128)} %rhs_in.1, f32[11,512]{1,0:T(8,128)} %pre_in.1, f32[1,512]{1,0:T(1,128)} %bitcast.7, s32[2,64]{1,0:T(2,128)} %halo_in.1, s32[4,2560]{1,0:T(4,128)} %conn_in.1, f32[3,4,2560]{2,1,0:T(4,128)} %grad_in.1, f32[5,2560]{1,0:T(8,128)} %coef_in.1, ...), custom_call_target="tpu_custom_call" | custom-call | tf_op jit(solution)/shard_map/pallas_call | solution.py:491
  48.1 0.0 copy-start
  48.1 1.4 %copy.19 = f32[11,512]{1,0:T(8,128)} copy(f32[11,512]{1,0:T(8,128)} %get-tuple-element.4) | data formatting | bytes 45056
  49.5 0.0 copy-done
  49.5 0.6 %copy.20 = f32[11,512]{1,0:T(8,128)} copy(f32[11,512]{1,0:T(8,128)S(1)} %copy-done) | data formatting | bytes 45056
  (3 shorter events, 0.1 us)
Async XLA Ops:
  0.6 0.9 %copy-start.1 = (f32[9,2,22]{2,1,0:T(2,128)S(1)}, f32[9,2,22]{2,1,0:T(2,128)}, u32[]{:S(2)}) copy-start(f32[9,2,22]{2,1,0:T(2,128)} %param.17) | copy-start | bytes 4756
  48.1 1.4 %copy-start = (f32[11,512]{1,0:T(8,128)S(1)}, f32[11,512]{1,0:T(8,128)}, u32[]{:S(2)}) copy-start(f32[11,512]{1,0:T(8,128)} %get-tuple-element.5) | copy-start | bytes 67588

commit v2 on v1

--- a/solution.py
+++ b/solution.py
@@ -53,28 +53,43 @@
     conn_in,
     grad_in,
     coef_in,
-    mix_in,
-    x_out,
-    res_out,
+    index_in,
+    value_in,
+    out,
     gathered,
     coefs,
+    mass_buf,
+    halo_buf,
+    conn,
+    grad,
+    index_buf,
+    value_buf,
     dstack,
     dsend,
     zinit,
     ids,
+    id_row,
     oht,
+    oh,
     halo_oh,
     base,
     mass_ext,
+    table,
+    stack,
     mix,
     sc_hi,
     sc_lo,
     loc,
+    mine_part,
+    from_k,
     part,
     from_x,
     from_z,
     dot_send,
     dot_recv,
+    last_send,
+    last_recv,
+    sem_in,
     sem_gs,
     sem_gr,
     sem_cs,
@@ -87,8 +102,12 @@
     sem_zr,
     sem_ds,
     sem_dr,
+    sem_ks,
+    sem_kr,
+    sem_ls,
+    sem_lr,
 ):
-    n_mesh, n_chaos, n_kl, modes, mode_dev, node, halo, elems, chunk, terms, term_dev = dims
+    n_mesh, n_chaos, n_kl, modes, mode_dev, node, halo, elems, terms, term_dev = dims
     rows = round_up(modes, 8)
     rd = round_up(mode_dev, 8)
     pairs = round_up(terms, 2)
@@ -113,22 +132,11 @@
     def greet(target):
         pl.semaphore_signal(barrier, inc=1, device_id=target, device_id_type=MESH)
 
-    for off in range(1, n_chaos):
-        greet({"chaos": peer_c(off)})
-    for off in range(1, n_mesh):
-        greet({"mesh": lax.rem(m + off, n_mesh)})
+    plane = [(a, b) for a in range(n_mesh) for b in range(n_chaos) if a or b]
+    for mesh_off, off in plane:
+        greet({"mesh": lax.rem(m + mesh_off, n_mesh), "chaos": peer_c(off)})
     for off in range(1, n_kl):
         greet({"kl": lax.rem(k + off, n_kl)})
-    for _, has, other in sides:
-        @pl.when(has)
-        def _():
-            for off in range(1, n_chaos):
-                greet({"mesh": other, "chaos": peer_c(off)})
-
-    neighbours = jnp.where(has_low, 1, 0) + jnp.where(has_up, 1, 0)
-    pl.semaphore_wait(
-        barrier, n_chaos - 1 + n_mesh - 1 + n_kl - 1 + neighbours * (n_chaos - 1)
-    )
 
     def remote(src, dst, send, recv, target):
         return pltpu.make_async_remote_copy(
@@ -136,23 +144,46 @@
             device_id=target, device_id_type=MESH,
         )
 
-    elem_at = pl.multiple_of(c * elems, 128)
-    mine = pl.ds(elem_at, elems)
+    def share(kl_index):
+        return pl.ds(pl.multiple_of((c * n_kl + kl_index) * elems, 128), elems)
+
+    mine = share(k)
     pending = []
-
-    coef_waits = []
-    for off in range(1, n_kl):
-        copy = remote(
-            coef_in.at[:, mine], coefs.at[k], sem_cs.at[off], sem_cr.at[off],
-            {"kl": lax.rem(k + off, n_kl)},
+    loads = [
+        pltpu.make_async_copy(src, dst, sem_in.at[at])
+        for at, (src, dst) in enumerate(
+            (
+                (halo_in, halo_buf),
+                (rhs_in, gathered.at[0, c]),
+                (pre_in, gathered.at[1, c]),
+                (mass_in, mass_buf),
+                (conn_in.at[:, mine], conn),
+                (index_in, index_buf),
+                (value_in, value_buf),
+                (grad_in.at[:, :, mine], grad),
+                (coef_in.at[:, mine], coefs.at[k]),
+            )
         )
-        copy.start()
-        pending.append((None, copy))
-        source = lax.rem(k + n_kl - off, n_kl)
-        coef_waits.append(
-            remote(coef_in.at[:, mine], coefs.at[source], sem_cs.at[off], sem_cr.at[off],
-                   {"kl": lax.rem(k + off, n_kl)})
-        )
+    ]
+    for load in loads:
+        load.start()
+    for load in loads[:4]:
+        load.wait()
+
+    hrow = jnp.concatenate([halo_buf[0:1, :], halo_buf[1:2, :]], axis=1)
+    sub = lax.broadcasted_iota(jnp.int32, (node, 2 * halo), 0)
+    hits = jnp.where(sub == hrow, 1.0, 0.0).astype(F32)
+    halo_oh[...] = hits.astype(BF16)
+    in_halo = jnp.sum(hits, axis=1, keepdims=True)
+
+    dstack[...] = jnp.zeros_like(dstack)
+    dstack[0:mode_dev, :] = gathered[0, c]
+    dstack[rd : rd + mode_dev, :] = gathered[1, c]
+    dstack[2 * rd : 2 * rd + 1, :] = mass_buf[...]
+    dsend[...] = fold(dot(split(dstack[...], 3), halo_oh[...]), dsend.shape[0])
+
+    pl.semaphore_wait(barrier, len(plane) + n_kl - 1)
+
     gather_waits = []
     for off in range(1, n_chaos):
         for which, ref in enumerate((rhs_in, pre_in)):
@@ -162,21 +193,6 @@
             copy.start()
             pending.append((None, copy))
             gather_waits.append(remote(ref, gathered.at[which, source_c(off)], *sems, target))
-    coefs[k] = coef_in[:, mine]
-    gathered[0, c] = rhs_in[...]
-    gathered[1, c] = pre_in[...]
-
-    hrow = jnp.concatenate([halo_in[0:1, :], halo_in[1:2, :]], axis=1)
-    sub = lax.broadcasted_iota(jnp.int32, (node, 2 * halo), 0)
-    hits = jnp.where(sub == hrow, 1.0, 0.0).astype(F32)
-    halo_oh[...] = hits.astype(BF16)
-    in_halo = jnp.sum(hits, axis=1, keepdims=True)
-
-    dstack[...] = jnp.zeros_like(dstack)
-    dstack[0:mode_dev, :] = rhs_in[...]
-    dstack[rd : rd + mode_dev, :] = pre_in[...]
-    dstack[2 * rd : 2 * rd + 1, :] = mass_in[...]
-    dsend[...] = fold(dot(split(dstack[...], 3), halo_oh[...]), dsend.shape[0])
 
     def to_sides(source_of, dst_of, send_of, recv_of):
         copies = []
@@ -210,7 +226,22 @@
                              sem_zir.at[side, off], target))
             )
 
+    coef_waits = []
+    for off in range(1, n_kl):
+        target = lax.rem(k + off, n_kl)
+        sems = (sem_cs.at[off], sem_cr.at[off])
+        copy = remote(coef_in.at[:, share(target)], coefs.at[k], *sems, {"kl": target})
+        copy.start()
+        pending.append((None, copy))
+        source = lax.rem(k + n_kl - off, n_kl)
+        coef_waits.append(
+            remote(coef_in.at[:, mine], coefs.at[source], *sems, {"kl": target})
+        )
+
     square = 2 * halo
+    lane = lax.broadcasted_iota(jnp.int32, (1, square), 1)
+    first_half = lane < halo
+    own_col = jnp.transpose(jnp.broadcast_to(in_halo, (node, 128)))[0:1]
     spread = jnp.broadcast_to(hrow.astype(F32), (square, square))
     columns = jnp.transpose(spread).astype(jnp.int32)
     ids[0:node, :] = jnp.where(in_halo > 0.0, -1, sub)
@@ -219,19 +250,58 @@
     ids[low_at + halo : up_at, :] = columns[:halo]
     ids[up_at : up_at + halo, :] = ghost + halo
     ids[up_at + halo : wide, :] = columns[halo:]
-
-    for corner in range(4):
-        for tile in range(elems // 128):
-            slots = conn_in[corner : corner + 1, pl.ds(elem_at + tile * 128, 128)]
-            at = corner * elems + tile * 128
+    node_lane = lax.broadcasted_iota(jnp.int32, (1, node), 1)
+    id_row[:, 0:node] = jnp.where(own_col > 0.0, -1, node_lane)
+    id_row[:, low_at:up_at] = jnp.where(first_half, node + lane, pltpu.roll(hrow, halo, 1))
+    id_row[:, up_at:wide] = jnp.where(first_half, node + halo + lane, hrow)
+
+    tiles = elems // 128
+    loads[4].wait()
+    for tile in range(tiles):
+        for corner in range(4):
+            slots = conn[corner : corner + 1, tile * 128 : (tile + 1) * 128]
+            at = (tile * 4 + corner) * 128
             oht[:, at : at + 128] = jnp.where(ids[...] == slots, 1.0, 0.0).astype(BF16)
-
-    mix[...] = split(mix_in[...], 2)
-    for buffer in range(2):
-        if pairs > terms:
-            sc_hi[buffer] = jnp.zeros_like(sc_hi[buffer])
-            sc_lo[buffer] = jnp.zeros_like(sc_lo[buffer])
-
+            down = jnp.transpose(jnp.broadcast_to(slots, (128, 128)))
+            for start in range(0, wide, 128):
+                there = slice(start, start + 128)
+                oh[at : at + 128, there] = jnp.where(
+                    down == id_row[:, there], 1.0, 0.0
+                ).astype(BF16)
+
+    loads[5].wait()
+    loads[6].wait()
+    table[...] = jnp.zeros_like(table)
+    stack[...] = jnp.zeros_like(stack)
+    packed = table.shape[2]
+    mode_sub = lax.broadcasted_iota(jnp.int32, (rows, stack.shape[1]), 0).astype(F32) + 1.0
+    flat = None
+    for term in range(terms):
+        table[term, 0:2, 0:modes] = index_buf[term].astype(F32) + 1.0
+        table[term, 2:4, 0:modes] = value_buf[term]
+        entry = table[term]
+        moved = pltpu.roll(entry, term * rows, 1) if term else entry
+        flat = moved if flat is None else flat + moved
+        block = None
+        for slot in range(2):
+            here = slice(0, stack.shape[1])
+            piece = jnp.where(
+                entry[slot : slot + 1, here] == mode_sub, entry[slot + 2 : slot + 3, here], 0.0
+            )
+            block = piece if block is None else block + piece
+        stack[term * rows : (term + 1) * rows, :] = block
+    both_ways = jnp.transpose(stack[...])[:rows]
+    flat_sub = lax.broadcasted_iota(jnp.int32, (rows, packed), 0).astype(F32) + 1.0
+    for slot in range(2):
+        both_ways = both_ways + jnp.where(
+            flat[slot : slot + 1] == flat_sub, flat[slot + 2 : slot + 3], 0.0
+        )
+    mix[...] = split(0.5 * both_ways, 2)
+    sc_hi[...] = jnp.zeros_like(sc_hi)
+    sc_lo[...] = jnp.zeros_like(sc_lo)
+
+    loads[7].wait()
+    loads[8].wait()
     for copy in coef_waits:
         copy.wait_recv()
     for copy in gather_waits:
@@ -239,9 +309,6 @@
     for has, copy in zinit_waits:
         pl.when(has)(copy.wait_recv)
 
-    lane = lax.broadcasted_iota(jnp.int32, (1, square), 1)
-    first_half = lane < halo
-    own_col = jnp.transpose(jnp.broadcast_to(in_halo, (node, 128)))[0:1]
     keep = jnp.where(own_col > 0.0, 0.0, 1.0)
 
     def blocks(dup, low, up):
@@ -270,7 +337,7 @@
     low, up = blocks(
         mass_dup, zinit[0, 0, 2 * rd : 2 * rd + 1, :], zinit[1, 0, 2 * rd : 2 * rd + 1, :]
     )
-    mass_ext[:, 0:node] = mass_in[...]
+    mass_ext[:, 0:node] = mass_buf[...]
     mass_ext[:, low_at:up_at] = low
     mass_ext[:, up_at:wide] = up
 
@@ -280,45 +347,57 @@
 
     def apply_local(vector, op):
         stacked = split(vector, 2)
-        for step in range(elems // chunk):
-            at = step * chunk
-            here = pl.ds(elem_at + at, chunk)
-            corners = [
-                fold(dot(stacked, oht[:, b * elems + at : b * elems + at + chunk]), rows)
-                for b in range(4)
-            ]
-            buffer = step % 2
-            main = []
+        main = []
+        for tile in range(tiles):
+            here = slice(tile * 128, (tile + 1) * 128)
+            picked = fold(dot(stacked, oht[:, tile * 512 : (tile + 1) * 512]), rows)
             for d in range(3):
-                projected = grad_in[d, 0:1, here] * corners[0]
-                for b in range(1, 4):
-                    projected = projected + grad_in[d, b : b + 1, here] * corners[b]
-                main.append(coefs[0, 0:1, at : at + chunk] * projected)
+                projected = None
+                for b in range(4):
+                    piece = grad[d, b : b + 1, here] * picked[:, b * 128 : (b + 1) * 128]
+                    projected = piece if projected is None else projected + piece
+                main.append(coefs[0, 0:1, here] * projected)
+                to = slice((tile * 3 + d) * 128, (tile * 3 + d + 1) * 128)
                 for first in range(1, terms + 1, 2):
                     pair = []
                     for term in range(first, min(first + 2, terms + 1)):
                         group, entry = divmod(term, term_dev)
-                        pair.append(coefs[group, entry : entry + 1, at : at + chunk] * projected)
+                        pair.append(coefs[group, entry : entry + 1, here] * projected)
                     while len(pair) < 2:
                         pair.append(jnp.zeros_like(projected))
                     both = jnp.concatenate(pair, axis=0)
                     high = both.astype(BF16)
-                    to = slice((first - 1) * rows, (first + 1) * rows)
-                    sc_hi[buffer, to, d * chunk : (d + 1) * chunk] = high
-                    sc_lo[buffer, to, d * chunk : (d + 1) * chunk] = (
-                        both - high.astype(F32)
-                    ).astype(BF16)
-            mixed = fold(dot(mix[...], sc_hi[buffer]), rows)
-            mixed = mixed + dot(mix[...], sc_lo[buffer])[:rows]
+                    down = slice((first - 1) * rows, (first + 1) * rows)
+                    sc_hi[down, to] = high
+                    sc_lo[down, to] = (both - high.astype(F32)).astype(BF16)
+        mixed = fold(dot(mix[...], sc_hi[...]), rows)
+        mixed = mixed + dot(mix[...], sc_lo[...])[:rows]
+        for tile in range(tiles):
+            here = slice(tile * 128, (tile + 1) * 128)
+            flows = [
+                main[tile * 3 + d] + mixed[:, (tile * 3 + d) * 128 : (tile * 3 + d + 1) * 128]
+                for d in range(3)
+            ]
             for a in range(4):
                 local = None
                 for d in range(3):
-                    piece = grad_in[d, a : a + 1, here] * (
-                        main[d] + mixed[:, d * chunk : (d + 1) * chunk]
-                    )
+                    piece = grad[d, a : a + 1, here] * flows[d]
                     local = piece if local is None else local + piece
-                loc[:, a * elems + at : a * elems + at + chunk] = split(local, 2)
-        part[op] = fold(dot_t(loc[...], oht[...]), rows)
+                at = (tile * 4 + a) * 128
+                loc[:, at : at + 128] = split(local, 2)
+        mine_part[op] = fold(dot(loc[...], oh[...]), rows)
+        copies = []
+        for off in range(1, n_kl):
+            copy = remote(mine_part.at[op], from_k.at[op, off], sem_ks.at[op, off],
+                          sem_kr.at[op, off], {"kl": lax.rem(k + off, n_kl)})
+            copy.start()
+            pending.append((None, copy))
+            copies.append(copy)
+        total = mine_part[op]
+        for off, copy in enumerate(copies, 1):
+            copy.wait_recv()
+            total = total + from_k[op, off]
+        part[op] = total
 
     def send_parts(op):
         arrivals = []
@@ -356,7 +435,7 @@
         return total + mass_ext[...] * vector
 
     def tile_sum(first, second):
-        product = first * second * counted
+        product = first * second
         total = None
         for row in range(0, rows, 8):
             for at in range(0, wide, 128):
@@ -365,8 +444,9 @@
         return total
 
     def send_dots(step, residual, image, shared):
-        dot_send[step, 0] = tile_sum(residual, shared)
-        dot_send[step, 1] = tile_sum(image, shared)
+        seen = shared * counted
+        dot_send[step, 0] = tile_sum(residual, seen)
+        dot_send[step, 1] = tile_sum(image, seen)
         dot_recv[step, m] = dot_send[step]
         arrivals = []
         for off in range(1, n_mesh):
@@ -385,11 +465,37 @@
         total = dot_recv[step, 0]
         for source in range(1, n_mesh):
             total = total + dot_recv[step, source]
+        return sum_both(total)
+
+    def sum_both(total):
         sums = [
             jnp.sum(jnp.sum(total[i], axis=0, keepdims=True), axis=1, keepdims=True)
             for i in range(2)
         ]
         return sums
+
+    def send_last(gamma_tile, delta_tile):
+        last_send[0] = gamma_tile
+        last_send[1] = delta_tile
+        last_recv[m * n_chaos + c] = last_send[...]
+        arrivals = []
+        for at, (mesh_off, off) in enumerate(plane):
+            target = {"mesh": lax.rem(m + mesh_off, n_mesh), "chaos": peer_c(off)}
+            sems = (sem_ls.at[at], sem_lr.at[at])
+            copy = remote(last_send, last_recv.at[m * n_chaos + c], *sems, target)
+            copy.start()
+            pending.append((None, copy))
+            source = lax.rem(m + n_mesh - mesh_off, n_mesh) * n_chaos + source_c(off)
+            arrivals.append(remote(last_send, last_recv.at[source], *sems, target))
+        return arrivals
+
+    def take_last(arrivals):
+        for copy in arrivals:
+            copy.wait_recv()
+        total = last_recv[0]
+        for source in range(1, n_mesh * n_chaos):
+            total = total + last_recv[source]
+        return sum_both(total)
 
     residual = base[0]
     pre = base[1]
@@ -400,13 +506,14 @@
     answer = None
     gamma_old = alpha_old = None
     for step in range(ITERS):
-        dots = send_dots(step, residual, image, shared)
         last = step == ITERS - 1
+        if step == 0 or not last:
+            dots = send_dots(step, residual, image, shared)
         scaled = pre * image
         if not last:
             apply_local(scaled, step + 1)
             arrivals = send_parts(step + 1)
-        gamma, delta = take_dots(step, dots)
+        gamma, delta = take_last(dots) if last and step else take_dots(step, dots)
         if step == 0:
             alpha = gamma / delta
             dir_pre, dir_res, direction = scaled, image, shared
@@ -420,13 +527,22 @@
             answer = answer + alpha * direction
         residual = residual - alpha * dir_res
         shared = shared - alpha * dir_pre
+        if step and step == ITERS - 2:
+            seen = shared * counted
+            rest = image - alpha * (beta * dir_image + mass_ext[...] * scaled)
+            first_group = jnp.where(c == 0, 1.0, 0.0).astype(F32)
+            dots = send_last(
+                first_group * tile_sum(residual, seen),
+                first_group * tile_sum(rest, seen)
+                - alpha * tile_sum(part[step + 1], shared),
+            )
         if not last:
             product = finish(scaled, step + 1, arrivals)
             dir_image = product if step == 0 else product + beta * dir_image
             image = image - alpha * dir_image
         gamma_old, alpha_old = gamma, alpha
 
-    for out, value in ((x_out, answer), (res_out, residual)):
+    for at, value in enumerate((answer, residual)):
         dup = jnp.where(
             first_half, pltpu.roll(value[:, low_at:up_at], halo, 1), value[:, up_at:wide]
         )
@@ -435,25 +551,13 @@
         for group in range(n_chaos):
             @pl.when(c == group)
             def _():
-                out[...] = base[0, group * mode_dev : (group + 1) * mode_dev, 0:node]
+                out[at] = base[0, group * mode_dev : (group + 1) * mode_dev, 0:node]
 
     for has, copy in pending:
         if has is None:
             copy.wait_send()
         else:
             pl.when(has)(copy.wait_send)
-
-
-def couple_terms(term_index, term_value, rows, pairs):
-    mode_count = term_index.shape[-1]
-    columns = lax.broadcasted_iota(jnp.int32, term_index.shape + (mode_count,), 3)
-    table = jnp.sum(
-        jnp.where(term_index[..., None] == columns, term_value[..., None], 0.0), axis=1
-    )
-    mirror = 0.5 * (table + jnp.swapaxes(table, 1, 2))
-    pad = rows - mode_count
-    mirror = jnp.pad(mirror, ((0, pairs - mirror.shape[0]), (0, pad), (0, pad)))
-    return jnp.transpose(mirror, (1, 0, 2)).reshape(rows, pairs * rows)
 
 
 def per_device(
@@ -475,44 +579,58 @@
     term_dev = coefficient.shape[0]
     terms = term_dev * n_kl - 1
     rows, rd, pairs = round_up(modes, 8), round_up(mode_dev, 8), round_up(terms, 2)
-    elems = round_up(-(-elem_dev // n_chaos), 128)
-    chunk = 256 if elems % 256 == 0 else 128
+    elems = round_up(-(-elem_dev // (n_chaos * n_kl)), 128)
     wide = node + 4 * halo
-    extra = elems * n_chaos - elem_dev
+    extra = elems * n_chaos * n_kl - elem_dev
     if extra:
         connectivity = jnp.pad(connectivity, ((0, 0), (0, extra)))
         gradients = jnp.pad(gradients, ((0, 0), (0, 0), (0, extra)))
         coefficient = jnp.pad(coefficient, ((0, 0), (0, extra)))
-    mix = couple_terms(term_index, term_value, rows, pairs)
-    dims = (n_mesh, n_chaos, n_kl, modes, mode_dev, node, halo, elems, chunk, terms, term_dev)
+    packed = round_up(pairs * rows, 128)
+    dims = (n_mesh, n_chaos, n_kl, modes, mode_dev, node, halo, elems, terms, term_dev)
     vmem = pltpu.VMEM
     dma = pltpu.SemaphoreType.DMA
     drows = 2 * rd + 8
-    return pl.pallas_call(
+    both = pl.pallas_call(
         functools.partial(kernel, dims),
-        out_shape=[jax.ShapeDtypeStruct((mode_dev, node), F32)] * 2,
-        in_specs=[pl.BlockSpec(memory_space=vmem)] * 8,
-        out_specs=[pl.BlockSpec(memory_space=vmem)] * 2,
+        out_shape=jax.ShapeDtypeStruct((2, mode_dev, node), F32),
+        in_specs=[pl.BlockSpec(memory_space=pl.ANY)] * 9,
+        out_specs=pl.BlockSpec(memory_space=vmem),
         scratch_shapes=[
             vmem((2, n_chaos, mode_dev, node), F32),
             vmem((n_kl, term_dev, elems), F32),
+            vmem((1, node), F32),
+            vmem((2, halo), jnp.int32),
+            vmem((4, elems), jnp.int32),
+            vmem((3, 4, elems), F32),
+            vmem(term_index.shape, jnp.int32),
+            vmem(term_value.shape, F32),
             vmem((drows, node), F32),
             vmem((drows, 2 * halo), F32),
             vmem((2, n_chaos, drows, 2 * halo), F32),
             vmem((wide, 2 * halo), jnp.int32),
+            vmem((1, wide), jnp.int32),
             vmem((wide, 4 * elems), BF16),
+            vmem((4 * elems, wide), BF16),
             vmem((node, 2 * halo), BF16),
             vmem((2, rows, wide), F32),
             vmem((1, wide), F32),
-            vmem((2 * rows, pairs * rows), BF16),
-            vmem((2, pairs * rows, 3 * chunk), BF16),
-            vmem((2, pairs * rows, 3 * chunk), BF16),
+            vmem((terms, 8, packed), F32),
+            vmem((packed, round_up(rows, 128)), F32),
+            vmem((2 * rows, packed), BF16),
+            vmem((packed, 3 * elems), BF16),
+            vmem((packed, 3 * elems), BF16),
             vmem((2 * rows, 4 * elems), BF16),
+            vmem((OPS, rows, wide), F32),
+            vmem((OPS, n_kl, rows, wide), F32),
             vmem((OPS, rows, wide), F32),
             vmem((OPS, n_chaos, rows, wide), F32),
             vmem((OPS, 2, n_chaos, rows, 2 * halo), F32),
             vmem((ITERS, 2, 8, 128), F32),
             vmem((ITERS, n_mesh, 2, 8, 128), F32),
+            vmem((2, 8, 128), F32),
+            vmem((n_mesh * n_chaos, 2, 8, 128), F32),
+            dma((9,)),
             dma((n_chaos, 2)),
             dma((n_chaos, 2)),
             dma((n_kl,)),
@@ -525,6 +643,10 @@
             dma((OPS, 2, n_chaos)),
             dma((ITERS, n_mesh)),
             dma((ITERS, n_mesh)),
+            dma((OPS, n_kl)),
+            dma((OPS, n_kl)),
+            dma((n_mesh * n_chaos,)),
+            dma((n_mesh * n_chaos,)),
         ],
         compiler_params=pltpu.CompilerParams(
             collective_id=0, has_side_effects=True, vmem_limit_bytes=56 * 2**20
@@ -537,8 +659,10 @@
         connectivity,
         gradients,
         coefficient,
-        mix,
+        term_index,
+        term_value,
     )
+    return both[0], both[1]
 
 
 def solution(mesh):

time: 50.3 us -> 35.7 us (0.71)
  Pallas kernels: 44.3 us -> 33.4 us
  local copies, waits for them, and re-layouts: 3.9 us -> 1.41 us
  other arithmetic: 1.18 us -> 0 us
    pallas_call x1, Pallas kernels: 44.3 us -> 33.4 us  [per_device(): pl.pallas_call(functools.partial(kernel, dims), out_shape=jax.ShapeDtypeS...]
    unnamed x8 -> x0, local copies, waits for them, and re-layouts: 3 us -> none
    squeeze x0 -> x1, local copies, waits for them, and re-layouts: none -> 1.41 us  [per_device(): return (both[0], both[1])]
    reduce_sum x1 -> x0, other arithmetic: 1.16 us -> none  [couple_terms(): jnp.sum(jnp.where(term_index[..., None] == columns, term_value[..., None]...]
    reshape x1 -> x0, local copies, waits for them, and re-layouts: 0.71 us -> none  [couple_terms(): return jnp.transpose(mirror, (1, 0, 2)).reshape(rows, pairs * rows)]
where the time goes in v2:
time: 35.7 us; the launch traced here: 35.5 us
  Pallas kernels  33.4 us (94%)
  local copies, waits for them, and re-layouts  1.41 us (4%)
  between operations  0.64 us (2%)
    pallas_call x1, Pallas kernels, per_device(): pl.pallas_call(functools.partial(kernel, dims), out_shape=jax.ShapeDtypeS...  33.4 us
    squeeze x1, local copies, waits for them, and re-layouts, per_device(): return (both[0], both[1])  1.41 us

profile of v2, /device:TPU:0, one launch (start us, length us, event | category | flops | bytes accessed | tf_op | source)
XLA Modules:
  0.0 35.5 jit_solution(10542635237745160587)
XLA Ops:
  0.6 33.4 %shard_map.104 = f32[2,11,512]{2,1,0:T(8,128)} custom-call(f32[11,512]{1,0:T(8,128)} %rhs_in.1, f32[11,512]{1,0:T(8,128)} %pre_in.1, f32[1,512]{1,0:T(1,128)} %bitcast.5, s32[2,64]{1,0:T(2,128)} %halo_in.1, s32[4,2560]{1,0:T(4,128)} %conn_in.1, f32[3,4,2560]{2,1,0:T(4,128)} %grad_in.1, f32[5,2560]{1,0:T(8,128)} %coef_in.1, s32[9,2,22]{2,1,0:T(2,128)} %index_in.1, ...), custom_call_target="tpu_custom_call" | custom-call | tf_op jit(solution)/shard_map/pallas_call | solution.py:594
  34.1 1.4 %slice_bitcast_fusion = (f32[11,512]{1,0:T(8,128)}, f32[11,512]{1,0:T(8,128)}) fusion(f32[2,11,512]{2,1,0:T(8,128)} %shard_map.104), kind=kLoop, calls=%fused_computation | loop fusion | bytes 90112 | tf_op jit(solution)/shard_map/squeeze | solution.py:665
